TPU v7x, 512 devices: a whole 4x4x16 slice. The times are simulated.
512 devices in a mesh: member: 16 (over z), mp: 32 (over x, y, core).
Axes of the slice: x: 4, y: 4, z: 16, core: 2. Of those that a mesh axis runs over, the one named last changes fastest.
Arguments:
- tokens: bfloat16 [16, 64, 64, 1024], P('member', 'mp'), may hold values from -6 to 6
- norm_gain: float32 [1024], replicated, may hold values from 0.5 to 8
- qkv_weight: bfloat16 [1024, 3072], P('mp'), may hold values from -0.1875 to 0.1875
- out_weight: bfloat16 [1024, 1024], P('mp'), may hold values from -0.1875 to 0.1875
- decode_weight: bfloat16 [1024, 90], replicated, may hold values from -0.1875 to 0.1875
- edges: int32 [64, 64, 16], P('mp'), may hold values from 0 to 4095, as said below
- truth: bfloat16 [90, 64, 64], P(None, 'mp', 'member'), may hold values from -6 to 6
Outputs:
- score: float32 [64, 64], P('mp', 'member')
- field_grad: float32 [16, 90, 64, 64], P('member', None, 'mp')
Inputs may be any that keep to these rules, and one draw needn't show every extreme that they name: edges[lat, lon, 0] is the node's own index lat * 64 + lon; every other edge of a node in latitude rows of band p (rows p * 2 to (p + 1) * 2 - 1) points to a node of band p - 1, p or p + 1.
All inputs are finite; a program needn't handle non-finite values.
Results may differ from a plain program's by a relative error of at most 0.0062.
The roundings to bfloat16 on the way count: a program that leaves them out, or rounds other values in their place, can miss the bound.
Values may be sent and summed in bfloat16 or wider, within the bound.
A program may use at most 64 MiB of HBM per device.

v0:
```python
import jax
import jax.numpy as jnp
from jax import lax
from jax.sharding import PartitionSpec as P

HEADS = 16


EPS = 1e-05


def extended(block, sides, width, periodic):
    for axis, dim in sides:
        count = lax.axis_size(axis)
        forward = [(i, i + 1) for i in range(count - 1)]
        if periodic:
            forward.append((count - 1, 0))
        backward = [(target, source) for source, target in forward]
        low = lax.ppermute(
            lax.slice_in_dim(block, block.shape[dim] - width, None, axis=dim), axis, forward
        )
        high = lax.ppermute(lax.slice_in_dim(block, 0, width, axis=dim), axis, backward)
        block = jnp.concatenate([low, block, high], axis=dim)
    return block


def rms_scale(values):
    return values * lax.rsqrt(jnp.mean(values * values, axis=-1, keepdims=True) + 1e-05)


def box_sum(grid):
    rows_sum = grid[..., :-2, :] + grid[..., 1:-1, :] + grid[..., 2:, :]
    return rows_sum[..., :-2] + rows_sum[..., 1:-1] + rows_sum[..., 2:]


def on_device(tokens, norm_gain, qkv_weight, out_weight, decode_weight, edges, truth):
    width = norm_gain.shape[0]
    lat_rows = tokens.shape[1]
    lon_all = tokens.shape[2]
    count = lat_rows * lon_all
    states = tokens.reshape(count, width).astype(jnp.float32)
    normed = (rms_scale(states) * norm_gain).astype(jnp.bfloat16)
    columns = normed
    qkv = jnp.dot(
        columns,
        lax.all_gather(qkv_weight, "mp", axis=0, tiled=True),
        preferred_element_type=jnp.float32,
    ).astype(jnp.bfloat16)
    query = qkv[:, :width]
    keyval = qkv[:, width:]
    window = extended(keyval, (("mp", 0),), count, False)
    offset = (lax.axis_index("mp") - 1) * count
    local_edges = edges.reshape(count, -1) - offset
    fan = local_edges.shape[1]
    head_size = width // HEADS
    block = 128

    def attend(args):
        query_block, edge_block = args
        gathered = jnp.take(window, edge_block, axis=0)
        keys = gathered[..., :width].reshape(block, fan, HEADS, head_size)
        values = gathered[..., width:].reshape(block, fan, HEADS, head_size)
        queries = query_block.reshape(block, HEADS, head_size)
        scores = jnp.einsum(
            "bhd,bkhd->bhk", queries, keys, preferred_element_type=jnp.float32
        ) * head_size ** (-0.5)
        top = jnp.max(scores, axis=-1, keepdims=True)
        expo = jnp.exp(scores - top)
        probs = (expo / jnp.sum(expo, axis=-1, keepdims=True)).astype(jnp.bfloat16)
        mixed = jnp.einsum("bhk,bkhd->bhd", probs, values, preferred_element_type=jnp.float32)
        return mixed.reshape(block, width).astype(jnp.bfloat16)

    attended = lax.map(
        attend,
        (
            query.reshape(count // block, block, width),
            local_edges.reshape(count // block, block, fan),
        ),
    ).reshape(count, width)
    columns = attended
    projected = jnp.dot(
        columns,
        lax.all_gather(out_weight, "mp", axis=0, tiled=True),
        preferred_element_type=jnp.float32,
    )
    state = states + projected
    field = jnp.dot(
        rms_scale(state).astype(jnp.bfloat16), decode_weight, preferred_element_type=jnp.float32
    ).astype(jnp.bfloat16)
    variables = field.shape[1]
    member_fields = field.T.reshape(1, variables, lat_rows, lon_all)
    truth_lead = truth[None]
    tiles = lax.all_to_all(member_fields, "member", split_axis=3, concat_axis=0, tiled=True)
    tiles_lat, truth_lat = (
        extended(tiles, (("mp", 2),), 1, False),
        extended(truth_lead, (("mp", 2),), 1, False),
    )
    tiles_ext, truth_ext = (
        extended(tiles_lat, (("member", 3),), 1, True),
        extended(truth_lat, (("member", 3),), 1, True),
    )
    fields_ext = tiles_ext.astype(jnp.float32)
    truth_f = truth_ext.astype(jnp.float32)
    members = fields_ext.shape[0]
    patch = 9.0 * variables
    to_truth = jnp.sum((fields_ext - truth_f) ** 2, axis=1)
    pair = jnp.sum((fields_ext[:, None] - fields_ext[None]) ** 2, axis=2)
    dist_truth = jnp.sqrt(box_sum(to_truth) / patch + EPS)
    dist_pair = jnp.sqrt(box_sum(pair) / patch + EPS)
    off_diag = (1.0 - jnp.eye(members, dtype=jnp.float32))[:, :, None, None]
    score = jnp.mean(dist_truth, axis=0) - jnp.sum(dist_pair * off_diag, axis=(0, 1)) / (
        2.0 * members * (members - 1)
    )
    coef_truth = 1.0 / dist_truth
    coef_pair = off_diag / ((members - 1) * dist_pair)
    tile_lat, tile_lon = (coef_truth.shape[1], coef_truth.shape[2])
    flat_pair = coef_pair.reshape(members * members, tile_lat, tile_lon)
    truth_lat_c, pair_lat_c = (
        extended(coef_truth, (("mp", 1),), 1, False),
        extended(flat_pair, (("mp", 1),), 1, False),
    )
    truth_full, pair_full = (
        extended(truth_lat_c, (("member", 2),), 1, True),
        extended(pair_lat_c, (("member", 2),), 1, True),
    )
    atot = box_sum(truth_full)
    btot = box_sum(pair_full).reshape(members, members, tile_lat, tile_lon)
    centre = fields_ext[:, :, 1:-1, 1:-1]
    truth_c = truth_f[:, :, 1:-1, 1:-1]
    grad_tile = atot[:, None] * (centre - truth_c) - jnp.sum(
        btot[:, :, None] * (centre[:, None] - centre[None]), axis=1
    )
    field_grad = lax.all_to_all(grad_tile, "member", split_axis=0, concat_axis=3, tiled=True)
    return (score, field_grad)


def solution(mesh):
    in_specs = (
        P("member", "mp", None, None),
        P(),
        P("mp", None),
        P("mp", None),
        P(),
        P("mp", None, None),
        P(None, "mp", "member"),
    )
    out_specs = (P("mp", "member"), P("member", None, "mp", None))
    return jax.shard_map(
        on_device, mesh=mesh, in_specs=in_specs, out_specs=out_specs, check_vma=False
    )
```

profile of v0, /device:TPU:6, one launch (start us, length us, event | category | flops | bytes accessed | tf_op | source)
XLA Modules:
  0.0 251.4 jit_solution(13809379398187574583)
XLA Ops:
  10.6 5.8 %collective-permute-start.7 = (bf16[1,90,1,4]{1,3,2,0:T(4,128)(2,1)S(1)}, bf16[1,90,1,4]{1,3,2,0:T(4,128)(2,1)S(1)}, u32[]{:S(2)}, u32[]{:S(2)}) collective-permute-start(bf16[1,90,1,4]{1,3,2,0:T(4,128)(2,1)S(1)} %get-tuple-element.41), channel_id=1, source_target_pairs={{1,0},{2,1},{3,2},{4,3},{5,4},{6,5},{7,6},{8,7},{9,8},{10,9},{11,1... | collective-permute-start | bytes 2168 | tf_op jit(solution)/shard_map/ppermute | solution.py:22
  19.7 59.5 %all-gather.3.cloned.1.call-done = bf16[1024,3072]{1,0:T(8,128)(2,1)} async-done(((bf16[32,3072]{1,0:T(8,128)(2,1)}), bf16[1024,3072]{1,0:T(8,128)(2,1)}) %all-gather.3.cloned.1.call-update) | async-done | bytes 6291472 | tf_op jit(solution)/shard_map/all_gather | solution.py:46
  79.2 3.8 %convolution_convert_fusion = bf16[128,3072]{1,0:T(8,128)(2,1)S(1)} fusion(bf16[128,1024]{1,0:T(8,128)(2,1)S(1)} %fusion.9, bf16[1024,3072]{1,0:T(8,128)(2,1)} %all-gather.3.cloned.1.call-done), kind=kOutput, calls=%fused_computation.6 | convolution fusion | flops 805699584 | bytes 7340032 | tf_op jit(solution)/shard_map/dot_general | solution.py:44
  85.2 5.5 %collective-permute-start.1 = (bf16[128,2048]{1,0:T(8,128)(2,1)S(1)}, bf16[128,2048]{1,0:T(8,128)(2,1)}, u32[]{:S(2)}, u32[]{:S(2)}) collective-permute-start(bf16[128,2048]{1,0:T(8,128)(2,1)S(1)} %slice.188), channel_id=1, source_target_pairs={{1,0},{2,1},{3,2},{4,3},{5,4},{6,5},{7,6},{8,7},{9,8},{10,9},{11,1... | collective-permute-start | bytes 1572872 | tf_op jit(solution)/shard_map/ppermute | solution.py:22
  91.1 4.6 %collective-permute-done = bf16[128,2048]{1,0:T(8,128)(2,1)S(1)} collective-permute-done((bf16[128,2048]{1,0:T(8,128)(2,1)S(1)}, bf16[128,2048]{1,0:T(8,128)(2,1)S(1)}, u32[]{:S(2)}, u32[]{:S(2)}) %collective-permute-start) | collective-permute-done | bytes 524320 | tf_op jit(solution)/shard_map/ppermute | solution.py:19
  98.6 11.0 %gather_fusion = bf16[2048,2048]{1,0:T(8,128)(2,1)} fusion(bf16[384,2048]{1,0:T(8,128)(2,1)S(1)} %pad_maximum_fusion, s32[2048]{0:T(1024)S(1)} %broadcast_clamp_fusion), kind=kCustom, calls=%fused_computation | custom fusion | bytes 16785408 | tf_op jit(solution)/shard_map/while/body/eval_jaxpr/jit(_take)/gather | solution.py:60
  109.6 12.5 %copy.129 = bf16[128,16,2048]{0,2,1:T(8,128)(2,1)} copy(bf16[128,16,2048]{2,1,0:T(8,128)(2,1)} %bitcast.53) | data formatting | bytes 16777216 | tf_op jit(solution)/shard_map/while/body/eval_jaxpr/jit(_take)/gather | solution.py:60
  122.1 7.4 %broadcast_select_fusion = bf16[128,16,2048]{0,2,1:T(8,128)(2,1)} fusion(bf16[128,16,2048]{0,2,1:T(8,128)(2,1)} %copy.129, pred[128,16]{0,1:T(8,128)(4,1)S(1)} %compare_and_fusion), kind=kLoop, calls=%fused_computation.5 | loop fusion | flops 4194304 | bytes 16779264 | tf_op jit(solution)/shard_map/while/body/eval_jaxpr/jit(_take)/select_n | solution.py:60
  129.5 5.2 %fusion.25 = (bf16[128,16,1024]{0,2,1:T(8,128)(2,1)S(1)}, bf16[128,16,1024]{0,2,1:T(8,128)(2,1)}) fusion(bf16[128,16,2048]{0,2,1:T(8,128)(2,1)} %broadcast_select_fusion), kind=kLoop, calls=%fused_computation.83 | loop fusion | bytes 16777216 | tf_op jit(solution)/shard_map/while/body/eval_jaxpr/slice | solution.py:61
  136.5 3.4 %multiply_reduce_fusion = bf16[128,16,64]{0,2,1:T(8,128)(2,1)S(1)} fusion(bf16[128,16,16,64]{0,3,1,2:T(8,128)(2,1)} %bitcast.54, f32[128,16,16]{0,1,2:T(8,128)S(1)} %copy.169), kind=kLoop, calls=%fused_computation.3 | loop fusion | flops 6160384 | bytes 4587520 | tf_op jit(solution)/shard_map/while/body/eval_jaxpr/bhk,bkhd->bhd/dot_general | solution.py:70
  144.2 12.3 %all-to-all-start = ((bf16[1,90,2,64]{1,2,0,3:T(2,128)(2,1)}), bf16[1,90,2,64]{1,2,0,3:T(2,128)(2,1)S(1)}, u32[]{:S(2)}, u32[]{:S(2)}) async-start(bf16[1,90,2,64]{1,2,0,3:T(2,128)(2,1)} %copy.131), calls=%async_computation | async-start | bytes 65536 | tf_op jit(solution)/shard_map/all_to_all | solution.py:93
  156.5 3.8 %collective-permute-start.8 = (bf16[1,90,4,1]{1,3,2,0:T(2,128)(2,1)S(1)}, bf16[1,90,4,1]{1,3,2,0:T(2,128)(2,1)S(1)}, u32[]{:S(2)}, u32[]{:S(2)}) collective-permute-start(bf16[1,90,4,1]{1,3,2,0:T(2,128)(2,1)S(1)} %get-tuple-element.38), channel_id=1, source_target_pairs={{0,32},{32,64},{64,96},{96,128},{128,160},{160,192},{192,224},{224... | collective-permute-start | bytes 2168 | tf_op jit(solution)/shard_map/ppermute | solution.py:19
  160.4 3.2 %collective-permute-start.9 = (bf16[1,90,4,1]{1,3,2,0:T(2,128)(2,1)S(1)}, bf16[1,90,4,1]{1,3,2,0:T(2,128)(2,1)S(1)}, u32[]{:S(2)}, u32[]{:S(2)}) collective-permute-start(bf16[1,90,4,1]{1,3,2,0:T(2,128)(2,1)S(1)} %get-tuple-element.39), channel_id=1, source_target_pairs={{32,0},{64,32},{96,64},{128,96},{160,128},{192,160},{224,192},{256... | collective-permute-start | bytes 2168 | tf_op jit(solution)/shard_map/ppermute | solution.py:22
  163.6 5.5 %all-to-all-done = bf16[1,90,2,64]{1,2,0,3:T(2,128)(2,1)S(1)} async-done(((bf16[1,90,2,64]{1,2,0,3:T(2,128)(2,1)}), bf16[1,90,2,64]{1,2,0,3:T(2,128)(2,1)S(1)}, u32[]{:S(2)}, u32[]{:S(2)}) %all-to-all-start) | async-done | bytes 23072 | tf_op jit(solution)/shard_map/all_to_all | solution.py:93
  171.0 5.8 %collective-permute-start.3 = (bf16[16,90,1,4]{1,3,2,0:T(4,128)(2,1)S(1)}, bf16[16,90,1,4]{1,3,2,0:T(4,128)(2,1)S(1)}, u32[]{:S(2)}, u32[]{:S(2)}) collective-permute-start(bf16[16,90,1,4]{1,3,2,0:T(4,128)(2,1)S(1)} %get-tuple-element.29), channel_id=1, source_target_pairs={{1,0},{2,1},{3,2},{4,3},{5,4},{6,5},{7,6},{8,7},{9,8},{10,9},{11,1... | collective-permute-start | bytes 34568 | tf_op jit(solution)/shard_map/ppermute | solution.py:22
  178.3 2.5 %collective-permute-start.4 = (bf16[16,90,4,1]{1,3,2,0:T(2,128)(2,1)S(1)}, bf16[16,90,4,1]{1,3,2,0:T(2,128)(2,1)S(1)}, u32[]{:S(2)}, u32[]{:S(2)}) collective-permute-start(bf16[16,90,4,1]{1,3,2,0:T(2,128)(2,1)S(1)} %get-tuple-element.21), channel_id=1, source_target_pairs={{0,32},{32,64},{64,96},{96,128},{128,160},{160,192},{192,224},{224... | collective-permute-start | bytes 34568 | tf_op jit(solution)/shard_map/ppermute | solution.py:19
  180.9 4.5 %collective-permute-start.5 = (bf16[16,90,4,1]{1,3,2,0:T(2,128)(2,1)S(1)}, bf16[16,90,4,1]{1,3,2,0:T(2,128)(2,1)S(1)}, u32[]{:S(2)}, u32[]{:S(2)}) collective-permute-start(bf16[16,90,4,1]{1,3,2,0:T(2,128)(2,1)S(1)} %get-tuple-element.22), channel_id=1, source_target_pairs={{32,0},{64,32},{96,64},{128,96},{160,128},{192,160},{224,192},{256... | collective-permute-start | bytes 34568 | tf_op jit(solution)/shard_map/ppermute | solution.py:22
  189.3 5.8 %collective-permute-start.11 = (f32[16,1,4]{2,0,1:T(8,128)S(1)}, f32[16,1,4]{2,0,1:T(8,128)S(1)}, u32[]{:S(2)}, u32[]{:S(2)}) collective-permute-start(f32[16,1,4]{2,0,1:T(8,128)S(1)} %get-tuple-element.31), channel_id=1, source_target_pairs={{1,0},{2,1},{3,2},{4,3},{5,4},{6,5},{7,6},{8,7},{9,8},{10,9},{11,1... | collective-permute-start | bytes 776 | tf_op jit(solution)/shard_map/ppermute | solution.py:22
  198.4 5.8 %collective-permute-start.15 = (f32[256,1,4]{0,2,1:T(4,128)S(1)}, f32[256,1,4]{0,2,1:T(4,128)S(1)}, u32[]{:S(2)}, u32[]{:S(2)}) collective-permute-start(f32[256,1,4]{0,2,1:T(4,128)S(1)} %get-tuple-element.36), channel_id=1, source_target_pairs={{1,0},{2,1},{3,2},{4,3},{5,4},{6,5},{7,6},{8,7},{9,8},{10,9},{11,1... | collective-permute-start | bytes 12296 | tf_op jit(solution)/shard_map/ppermute | solution.py:22
  204.4 2.5 collective-permute-start.12
  206.9 4.9 %collective-permute-start.13 = (f32[16,4,1]{2,0,1:T(8,128)S(1)}, f32[16,4,1]{2,0,1:T(8,128)S(1)}, u32[]{:S(2)}, u32[]{:S(2)}) collective-permute-start(f32[16,4,1]{2,0,1:T(8,128)S(1)} %get-tuple-element.24), channel_id=1, source_target_pairs={{32,0},{64,32},{96,64},{128,96},{160,128},{192,160},{224,192},{256... | collective-permute-start | bytes 776 | tf_op jit(solution)/shard_map/ppermute | solution.py:22
  215.6 5.4 %collective-permute-start.17 = (f32[256,4,1]{0,2,1:T(1,128)S(1)}, f32[256,4,1]{0,2,1:T(1,128)S(1)}, u32[]{:S(2)}, u32[]{:S(2)}) collective-permute-start(f32[256,4,1]{0,2,1:T(1,128)S(1)} %get-tuple-element.34), channel_id=1, source_target_pairs={{32,0},{64,32},{96,64},{128,96},{160,128},{192,160},{224,192},{256... | collective-permute-start | bytes 12296 | tf_op jit(solution)/shard_map/ppermute | solution.py:22
  223.7 7.4 %all-to-all-start.1 = ((f32[16,90,2,4]{1,3,2,0:T(4,128)}), f32[16,90,2,4]{1,3,2,0:T(4,128)S(1)}, u32[]{:S(2)}, u32[]{:S(2)}) async-start(f32[16,90,2,4]{1,3,2,0:T(4,128)} %multiply_subtract_fusion), calls=%async_computation.1 | async-start | bytes 131072 | tf_op jit(solution)/shard_map/all_to_all | solution.py:133
  231.6 12.3 %all-to-all-done.1 = f32[16,90,2,4]{1,3,2,0:T(4,128)S(1)} async-done(((f32[16,90,2,4]{1,3,2,0:T(4,128)}), f32[16,90,2,4]{1,3,2,0:T(4,128)S(1)}, u32[]{:S(2)}, u32[]{:S(2)}) %all-to-all-start.1) | async-done | bytes 46112 | tf_op jit(solution)/shard_map/all_to_all | solution.py:133
  (111 shorter events, 36.6 us)
Async XLA Ops:
  7.2 136.0 %copy-start = (bf16[1024,90]{0,1:T(8,128)(2,1)S(1)}, bf16[1024,90]{0,1:T(8,128)(2,1)}, u32[]{:S(2)}) copy-start(bf16[1024,90]{0,1:T(8,128)(2,1)} %param.11) | copy-start | bytes 552964
  7.2 72.0 %all-gather.3.cloned.1.call-start = ((), (), s32[]{:S(2)}) async-start(), calls=%async_computation.2 | async-start | bytes 6488064 | tf_op jit(solution)/shard_map/all_gather | solution.py:46
  7.9 133.0 %all-gather.5.cloned.1.call-start = ((), (), s32[]{:S(2)}) async-start(), calls=%async_computation.3 | async-start | bytes 2162688 | tf_op jit(solution)/shard_map/all_gather | solution.py:83
  8.7 82.1 %collective-permute-start.6 = (bf16[1,90,1,4]{1,3,2,0:T(4,128)(2,1)S(1)}, bf16[1,90,1,4]{1,3,2,0:T(4,128)(2,1)S(1)}, u32[]{:S(2)}, u32[]{:S(2)}) collective-permute-start(bf16[1,90,1,4]{1,3,2,0:T(4,128)(2,1)S(1)} %get-tuple-element.40), channel_id=1, source_target_pairs={{0,1},{1,2},{2,3},{3,4},{4,5},{5,6},{6,7},{7,8},{8,9},{9,10},{10,1... | collective-permute-start | bytes 2168 | tf_op jit(solution)/shard_map/ppermute | solution.py:19
  10.6 80.2 %collective-permute-start.7 = (bf16[1,90,1,4]{1,3,2,0:T(4,128)(2,1)S(1)}, bf16[1,90,1,4]{1,3,2,0:T(4,128)(2,1)S(1)}, u32[]{:S(2)}, u32[]{:S(2)}) collective-permute-start(bf16[1,90,1,4]{1,3,2,0:T(4,128)(2,1)S(1)} %get-tuple-element.41), channel_id=1, source_target_pairs={{1,0},{2,1},{3,2},{4,3},{5,4},{6,5},{7,6},{8,7},{9,8},{10,9},{11,1... | collective-permute-start | bytes 2168 | tf_op jit(solution)/shard_map/ppermute | solution.py:22
  19.7 71.0 %copy-start.2 = (bf16[90,2,4]{0,2,1:T(4,128)(2,1)S(1)}, bf16[90,2,4]{0,2,1:T(4,128)(2,1)}, u32[]{:S(2)}) copy-start(bf16[90,2,4]{0,2,1:T(4,128)(2,1)} %param.13) | copy-start | bytes 4324
  83.1 12.6 %collective-permute-start = (bf16[128,2048]{1,0:T(8,128)(2,1)S(1)}, bf16[128,2048]{1,0:T(8,128)(2,1)S(1)}, u32[]{:S(2)}, u32[]{:S(2)}) collective-permute-start(bf16[128,2048]{1,0:T(8,128)(2,1)S(1)} %slice.188), channel_id=1, source_target_pairs={{0,1},{1,2},{2,3},{3,4},{4,5},{5,6},{6,7},{7,8},{8,9},{9,10},{10,1... | collective-permute-start | bytes 1572872 | tf_op jit(solution)/shard_map/ppermute | solution.py:19
  85.2 12.2 %collective-permute-start.1 = (bf16[128,2048]{1,0:T(8,128)(2,1)S(1)}, bf16[128,2048]{1,0:T(8,128)(2,1)}, u32[]{:S(2)}, u32[]{:S(2)}) collective-permute-start(bf16[128,2048]{1,0:T(8,128)(2,1)S(1)} %slice.188), channel_id=1, source_target_pairs={{1,0},{2,1},{3,2},{4,3},{5,4},{6,5},{7,6},{8,7},{9,8},{10,9},{11,1... | collective-permute-start | bytes 1572872 | tf_op jit(solution)/shard_map/ppermute | solution.py:22
  144.2 24.9 %all-to-all-start = ((bf16[1,90,2,64]{1,2,0,3:T(2,128)(2,1)}), bf16[1,90,2,64]{1,2,0,3:T(2,128)(2,1)S(1)}, u32[]{:S(2)}, u32[]{:S(2)}) async-start(bf16[1,90,2,64]{1,2,0,3:T(2,128)(2,1)} %copy.131), calls=%async_computation | async-start | bytes 65536 | tf_op jit(solution)/shard_map/all_to_all | solution.py:93
  156.5 28.9 %collective-permute-start.8 = (bf16[1,90,4,1]{1,3,2,0:T(2,128)(2,1)S(1)}, bf16[1,90,4,1]{1,3,2,0:T(2,128)(2,1)S(1)}, u32[]{:S(2)}, u32[]{:S(2)}) collective-permute-start(bf16[1,90,4,1]{1,3,2,0:T(2,128)(2,1)S(1)} %get-tuple-element.38), channel_id=1, source_target_pairs={{0,32},{32,64},{64,96},{96,128},{128,160},{160,192},{192,224},{224... | collective-permute-start | bytes 2168 | tf_op jit(solution)/shard_map/ppermute | solution.py:19
  160.4 25.1 %collective-permute-start.9 = (bf16[1,90,4,1]{1,3,2,0:T(2,128)(2,1)S(1)}, bf16[1,90,4,1]{1,3,2,0:T(2,128)(2,1)S(1)}, u32[]{:S(2)}, u32[]{:S(2)}) collective-permute-start(bf16[1,90,4,1]{1,3,2,0:T(2,128)(2,1)S(1)} %get-tuple-element.39), channel_id=1, source_target_pairs={{32,0},{64,32},{96,64},{128,96},{160,128},{192,160},{224,192},{256... | collective-permute-start | bytes 2168 | tf_op jit(solution)/shard_map/ppermute | solution.py:22
  169.1 7.7 %collective-permute-start.2 = (bf16[16,90,1,4]{1,3,2,0:T(4,128)(2,1)S(1)}, bf16[16,90,1,4]{1,3,2,0:T(4,128)(2,1)S(1)}, u32[]{:S(2)}, u32[]{:S(2)}) collective-permute-start(bf16[16,90,1,4]{1,3,2,0:T(4,128)(2,1)S(1)} %get-tuple-element.28), channel_id=1, source_target_pairs={{0,1},{1,2},{2,3},{3,4},{4,5},{5,6},{6,7},{7,8},{8,9},{9,10},{10,1... | collective-permute-start | bytes 34568 | tf_op jit(solution)/shard_map/ppermute | solution.py:19
  171.0 7.2 %collective-permute-start.3 = (bf16[16,90,1,4]{1,3,2,0:T(4,128)(2,1)S(1)}, bf16[16,90,1,4]{1,3,2,0:T(4,128)(2,1)S(1)}, u32[]{:S(2)}, u32[]{:S(2)}) collective-permute-start(bf16[16,90,1,4]{1,3,2,0:T(4,128)(2,1)S(1)} %get-tuple-element.29), channel_id=1, source_target_pairs={{1,0},{2,1},{3,2},{4,3},{5,4},{6,5},{7,6},{8,7},{9,8},{10,9},{11,1... | collective-permute-start | bytes 34568 | tf_op jit(solution)/shard_map/ppermute | solution.py:22
  178.3 7.1 %collective-permute-start.4 = (bf16[16,90,4,1]{1,3,2,0:T(2,128)(2,1)S(1)}, bf16[16,90,4,1]{1,3,2,0:T(2,128)(2,1)S(1)}, u32[]{:S(2)}, u32[]{:S(2)}) collective-permute-start(bf16[16,90,4,1]{1,3,2,0:T(2,128)(2,1)S(1)} %get-tuple-element.21), channel_id=1, source_target_pairs={{0,32},{32,64},{64,96},{96,128},{128,160},{160,192},{192,224},{224... | collective-permute-start | bytes 34568 | tf_op jit(solution)/shard_map/ppermute | solution.py:19
  180.9 6.1 %collective-permute-start.5 = (bf16[16,90,4,1]{1,3,2,0:T(2,128)(2,1)S(1)}, bf16[16,90,4,1]{1,3,2,0:T(2,128)(2,1)S(1)}, u32[]{:S(2)}, u32[]{:S(2)}) collective-permute-start(bf16[16,90,4,1]{1,3,2,0:T(2,128)(2,1)S(1)} %get-tuple-element.22), channel_id=1, source_target_pairs={{32,0},{64,32},{96,64},{128,96},{160,128},{192,160},{224,192},{256... | collective-permute-start | bytes 34568 | tf_op jit(solution)/shard_map/ppermute | solution.py:22
  187.4 16.9 %collective-permute-start.10 = (f32[16,1,4]{2,0,1:T(8,128)S(1)}, f32[16,1,4]{2,0,1:T(8,128)S(1)}, u32[]{:S(2)}, u32[]{:S(2)}) collective-permute-start(f32[16,1,4]{2,0,1:T(8,128)S(1)} %get-tuple-element.30), channel_id=1, source_target_pairs={{0,1},{1,2},{2,3},{3,4},{4,5},{5,6},{6,7},{7,8},{8,9},{9,10},{10,1... | collective-permute-start | bytes 776 | tf_op jit(solution)/shard_map/ppermute | solution.py:19
  189.3 15.0 %collective-permute-start.11 = (f32[16,1,4]{2,0,1:T(8,128)S(1)}, f32[16,1,4]{2,0,1:T(8,128)S(1)}, u32[]{:S(2)}, u32[]{:S(2)}) collective-permute-start(f32[16,1,4]{2,0,1:T(8,128)S(1)} %get-tuple-element.31), channel_id=1, source_target_pairs={{1,0},{2,1},{3,2},{4,3},{5,4},{6,5},{7,6},{8,7},{9,8},{10,9},{11,1... | collective-permute-start | bytes 776 | tf_op jit(solution)/shard_map/ppermute | solution.py:22
  196.5 17.0 %collective-permute-start.14 = (f32[256,1,4]{0,2,1:T(4,128)S(1)}, f32[256,1,4]{0,2,1:T(4,128)S(1)}, u32[]{:S(2)}, u32[]{:S(2)}) collective-permute-start(f32[256,1,4]{0,2,1:T(4,128)S(1)} %get-tuple-element.37), channel_id=1, source_target_pairs={{0,1},{1,2},{2,3},{3,4},{4,5},{5,6},{6,7},{7,8},{8,9},{9,10},{10,1... | collective-permute-start | bytes 12296 | tf_op jit(solution)/shard_map/ppermute | solution.py:19
  198.4 15.1 %collective-permute-start.15 = (f32[256,1,4]{0,2,1:T(4,128)S(1)}, f32[256,1,4]{0,2,1:T(4,128)S(1)}, u32[]{:S(2)}, u32[]{:S(2)}) collective-permute-start(f32[256,1,4]{0,2,1:T(4,128)S(1)} %get-tuple-element.36), channel_id=1, source_target_pairs={{1,0},{2,1},{3,2},{4,3},{5,4},{6,5},{7,6},{8,7},{9,8},{10,9},{11,1... | collective-permute-start | bytes 12296 | tf_op jit(solution)/shard_map/ppermute | solution.py:22
  204.4 7.5 %collective-permute-start.12 = (f32[16,4,1]{2,0,1:T(8,128)S(1)}, f32[16,4,1]{2,0,1:T(8,128)S(1)}, u32[]{:S(2)}, u32[]{:S(2)}) collective-permute-start(f32[16,4,1]{2,0,1:T(8,128)S(1)} %get-tuple-element.23), channel_id=1, source_target_pairs={{0,32},{32,64},{64,96},{96,128},{128,160},{160,192},{192,224},{224... | collective-permute-start | bytes 776 | tf_op jit(solution)/shard_map/ppermute | solution.py:19
  206.9 6.5 %collective-permute-start.13 = (f32[16,4,1]{2,0,1:T(8,128)S(1)}, f32[16,4,1]{2,0,1:T(8,128)S(1)}, u32[]{:S(2)}, u32[]{:S(2)}) collective-permute-start(f32[16,4,1]{2,0,1:T(8,128)S(1)} %get-tuple-element.24), channel_id=1, source_target_pairs={{32,0},{64,32},{96,64},{128,96},{160,128},{192,160},{224,192},{256... | collective-permute-start | bytes 776 | tf_op jit(solution)/shard_map/ppermute | solution.py:22
  213.5 7.5 %collective-permute-start.16 = (f32[256,4,1]{0,2,1:T(1,128)S(1)}, f32[256,4,1]{0,2,1:T(1,128)S(1)}, u32[]{:S(2)}, u32[]{:S(2)}) collective-permute-start(f32[256,4,1]{0,2,1:T(1,128)S(1)} %get-tuple-element.35), channel_id=1, source_target_pairs={{0,32},{32,64},{64,96},{96,128},{128,160},{160,192},{192,224},{224... | collective-permute-start | bytes 12296 | tf_op jit(solution)/shard_map/ppermute | solution.py:19
  215.6 6.7 %collective-permute-start.17 = (f32[256,4,1]{0,2,1:T(1,128)S(1)}, f32[256,4,1]{0,2,1:T(1,128)S(1)}, u32[]{:S(2)}, u32[]{:S(2)}) collective-permute-start(f32[256,4,1]{0,2,1:T(1,128)S(1)} %get-tuple-element.34), channel_id=1, source_target_pairs={{32,0},{64,32},{96,64},{128,96},{160,128},{192,160},{224,192},{256... | collective-permute-start | bytes 12296 | tf_op jit(solution)/shard_map/ppermute | solution.py:22
  223.7 20.2 %all-to-all-start.1 = ((f32[16,90,2,4]{1,3,2,0:T(4,128)}), f32[16,90,2,4]{1,3,2,0:T(4,128)S(1)}, u32[]{:S(2)}, u32[]{:S(2)}) async-start(f32[16,90,2,4]{1,3,2,0:T(4,128)} %multiply_subtract_fusion), calls=%async_computation.1 | async-start | bytes 131072 | tf_op jit(solution)/shard_map/all_to_all | solution.py:133
  (1 other events, 6.3 us)
Sparse Core Ops, SparseCore 0:
  11.1 68.0 all-gather.2
  82.4 58.5 all-gather.4
where the time goes:
time: 253 us; the launch traced here: 251 us
  waiting for transfers between devices  90.8 us (36%)
  starting transfers between devices  86.9 us (34%)
  local copies, waits for them, and re-layouts  32.5 us (13%)
  other arithmetic  20.3 us (8%)
  between operations  14.7 us (6%)
  matrix products  6.2 us (2%)
    all_gather x1, waiting for transfers between devices, on_device(): lax.all_gather(qkv_weight, 'mp', axis=0, tiled=True)  59.5 us
    ppermute x9, starting transfers between devices, extended(): lax.ppermute(lax.slice_in_dim(block, 0, width, axis=dim), axis, backward)  46.6 us
    gather x2, local copies, waits for them, and re-layouts, attend(): gathered = jnp.take(window, edge_block, axis=0)  23.5 us
    ppermute x9, starting transfers between devices, extended(): lax.ppermute(lax.slice_in_dim(block, block.shape[dim] - width, None, axis...  20.6 us
    all_to_all x1, starting transfers between devices, on_device(): lax.all_to_all(member_fields, 'member', split_axis=3, concat_axis=0, tile...  12.3 us
    all_to_all x1, waiting for transfers between devices, on_device(): lax.all_to_all(grad_tile, 'member', split_axis=0, concat_axis=3, tiled=True)  12.3 us
    select_n x2, other arithmetic, attend(): gathered = jnp.take(window, edge_block, axis=0)  7.39 us
    all_to_all x1, starting transfers between devices, on_device(): lax.all_to_all(grad_tile, 'member', split_axis=0, concat_axis=3, tiled=True)  7.37 us
  transfers between devices with their start and end apart: 22, of which 10 were waited for; matrix products, arithmetic and copies ran while one was open for 21% of the time, Pallas kernels for 0%

commit v1 on v0

v1 whole, which is shorter than its diff:
```python
import jax
import jax.numpy as jnp
from jax import lax
from jax.experimental import pallas as pl
from jax.experimental.pallas import tpu as pltpu
from jax.sharding import PartitionSpec as P

MESH = pl.DeviceIdType.MESH
F32, BF16 = jnp.float32, jnp.bfloat16
EPS = 1e-05
NX, NY, NC = 4, 4, 2
MEMBERS = 16
BANDS = NX * NY * NC
TOK = 128
WIN = 3 * TOK
D = 1024
V = 90
VP = 96
FAN = 16
HEADS_C = 4
QKV_CHUNKS = 4
CHUNKS = QKV_CHUNKS + 1
COLS = 256
STEPS = 17
LANES = MEMBERS * 16
PATCH = 9.0 * V


def iota(shape, dim):
    return lax.broadcasted_iota(jnp.int32, shape, dim)


def hot(mask, dtype=BF16):
    return jnp.where(mask, 1.0, 0.0).astype(dtype)


def dot(a, b, **kw):
    return jnp.dot(a, b, preferred_element_type=F32, **kw)


def dot_t(a, b, **kw):
    return lax.dot_general(a, b, (((1,), (1,)), ((), ())), preferred_element_type=F32, **kw)


def rms_scale(v):
    return v * lax.rsqrt(jnp.mean(v * v, axis=-1, keepdims=True) + EPS)


def kernel(
    tok_ref, gain_ref, wqkv_ref, wout_ref, dec_ref, edge_ref, truth_ref,
    score_ref, grad_ref,
    wq, wo, halo, normed, count, att, stage, recv, trec, e_all, gsend, grecv,
    w_ssem, w_rsem, h_ssem, h_rsem, t_ssem, t_rsem, a_ssem, a_rsem, e_ssem, e_rsem, g_ssem, g_rsem,
):
    z = lax.axis_index("member")
    p = lax.axis_index("mp")
    x, y, c = lax.div(p, NY * NC), lax.rem(lax.div(p, NC), NY), lax.rem(p, NC)
    xm, xp, x2 = lax.rem(x + 3, NX), lax.rem(x + 1, NX), lax.rem(x + 2, NX)
    ym, yp, y2 = lax.rem(y + 3, NY), lax.rem(y + 1, NY), lax.rem(y + 2, NY)

    def chip(cx, cy, cc):
        return (z, (cx * NY + cy) * NC + cc)

    at_xp, at_xm, at_yp, at_ym = chip(xp, y, c), chip(xm, y, c), chip(x, yp, c), chip(x, ym, c)
    sib = chip(x, y, 1 - c)
    low, high = (z, lax.rem(p + BANDS - 1, BANDS)), (z, lax.rem(p + 1, BANDS))

    def other(k):
        return lax.rem(z + k, MEMBERS)

    barrier = pltpu.get_barrier_semaphore()
    partners = [at_xp, at_xm, at_yp, at_ym, sib, low, high]
    for target in partners:
        pl.semaphore_signal(barrier, inc=1, device_id=target, device_id_type=MESH)
    for k in range(1, MEMBERS):
        pl.semaphore_signal(barrier, inc=1, device_id=(other(k), p), device_id_type=MESH)

    for j in range(QKV_CHUNKS):
        for part in range(3):
            wq[j, x, y, c, :, part * COLS : (part + 1) * COLS] = wqkv_ref[
                :, part * D + j * COLS : part * D + (j + 1) * COLS
            ]
    wo[x, y, c] = wout_ref[...]
    pl.semaphore_wait(barrier, len(partners) + MEMBERS - 1)

    sent = []

    def send(src, dst, ssem, rsem, target):
        copy = pltpu.make_async_remote_copy(
            src_ref=src, dst_ref=dst, send_sem=ssem, recv_sem=rsem, device_id=target, device_id_type=MESH
        )
        copy.start()
        sent.append(copy)

    def arrive(dst, ssem, rsem):
        pltpu.make_async_remote_copy(
            src_ref=dst, dst_ref=dst, send_sem=ssem, recv_sem=rsem, device_id=sib, device_id_type=MESH
        ).wait_recv()

    def buf(j):
        return (wq.at[j], 3 * COLS) if j < QKV_CHUNKS else (wo, D)

    A, B = pl.ds(0, 16), pl.ds(16, 16)
    ALL = slice(None)

    def pieces(j):
        _, n = buf(j)
        lo, hi = pl.ds(0, n // 2), pl.ds(n // 2, n // 2)
        return [
            ((x, y, c, A), at_xp, (xm, y, c, A)),
            ((x, y, c, A), at_xm, (xp, y, c, A)),
            ((x, y, c, B), at_yp, (x, ym, c, B)),
            ((x, y, c, B), at_ym, (x, yp, c, B)),
            ((xm, y, c, A, lo), at_xp, (x2, y, c, A, lo)),
            ((xp, y, c, A, hi), at_xm, (x2, y, c, A, hi)),
            ((x, ym, c, B, lo), at_yp, (x, y2, c, B, lo)),
            ((x, yp, c, B, hi), at_ym, (x, y2, c, B, hi)),
            ((ALL, y, c, A), at_yp, (ALL, ym, c, A)),
            ((ALL, y, c, A), at_ym, (ALL, yp, c, A)),
            ((x, ALL, c, B), at_xp, (xm, ALL, c, B)),
            ((x, ALL, c, B), at_xm, (xp, ALL, c, B)),
            ((ALL, ym, c, A, lo), at_yp, (ALL, y2, c, A, lo)),
            ((ALL, yp, c, A, hi), at_ym, (ALL, y2, c, A, hi)),
            ((xm, ALL, c, B, lo), at_xp, (x2, ALL, c, B, lo)),
            ((xp, ALL, c, B, hi), at_xm, (x2, ALL, c, B, hi)),
            ((ALL, ALL, c), sib, (ALL, ALL, 1 - c)),
        ]

    def go(j, first, last):
        ref, _ = buf(j)
        for i in range(first, last):
            src, target, _ = pieces(j)[i]
            send(ref.at[src], ref.at[src], w_ssem.at[j, i], w_rsem.at[j, i], target)

    def got(j, first, last):
        ref, _ = buf(j)
        for i in range(first, last):
            arrive(ref.at[pieces(j)[i][2]], w_ssem.at[j, i], w_rsem.at[j, i])

    go(0, 0, 4)
    send(tok_ref, halo.at[1], h_ssem.at[1], h_rsem.at[1], low)
    send(tok_ref, halo.at[0], h_ssem.at[0], h_rsem.at[0], high)
    for j in range(1, CHUNKS):
        go(j, 0, 4)

    eye90 = hot(iota((V, TOK), 0) == iota((V, TOK), 1))
    truth_t = lax.dot_general(truth_ref[...], eye90, (((0,), (0,)), ((), ())), preferred_element_type=F32)
    trec[1] = jnp.concatenate([truth_t, jnp.zeros_like(truth_t)], axis=0).astype(BF16)
    send(trec.at[1], trec.at[0], t_ssem.at[0], t_rsem.at[0], (other(1), p))
    send(trec.at[1], trec.at[2], t_ssem.at[1], t_rsem.at[1], (other(MEMBERS - 1), p))

    def norm(rows):
        return (rms_scale(rows[...].astype(F32)) * gain_ref[...]).astype(BF16)

    normed[TOK : 2 * TOK] = norm(tok_ref)
    local = edge_ref[...] - (p - 1) * TOK
    nodes = iota((TOK, WIN), 1)
    total = jnp.zeros((TOK, WIN), F32)
    for k in range(FAN):
        total += jnp.where(local[:, k : k + 1] == nodes, 1.0, 0.0)
    count[...] = total

    def heads(j):
        weight = wq[j].reshape(D, 3 * COLS)
        query = dot(normed[TOK : 2 * TOK], weight[:, :COLS]).astype(BF16)
        keyval = dot(normed[...], weight[:, COLS:]).astype(BF16)
        key, value = keyval[:, :COLS], keyval[:, COLS:]
        head_of = iota((TOK, COLS), 1) >> 6
        spread = jnp.concatenate(
            [jnp.where(head_of == h, query, jnp.zeros_like(query)) for h in range(HEADS_C)], axis=0
        )
        scores = dot_t(spread, key) * 0.125
        times = count[...]
        probs = []
        for h in range(HEADS_C):
            s = jnp.where(times > 0.0, scores[h * TOK : (h + 1) * TOK], -1e30)
            expo = jnp.exp(s - jnp.max(s, axis=-1, keepdims=True)) * times
            probs.append((expo * (1.0 / jnp.sum(expo, axis=-1, keepdims=True))).astype(BF16))
        mixed = dot(jnp.concatenate(probs, axis=0), value)
        out = jnp.zeros((TOK, COLS), F32)
        for h in range(HEADS_C):
            out = jnp.where(head_of == h, mixed[h * TOK : (h + 1) * TOK], out)
        att[:, j * COLS : (j + 1) * COLS] = out.astype(BF16)

    for tick in range(CHUNKS + 4):
        j = tick
        if j < CHUNKS:
            got(j, 0, 4)
            go(j, 4, 8)
        j = tick - 1
        if 0 <= j < CHUNKS:
            got(j, 4, 8)
            go(j, 8, 12)
        j = tick - 2
        if 0 <= j < CHUNKS:
            got(j, 8, 12)
            go(j, 12, 16)
        j = tick - 3
        if 0 <= j < CHUNKS:
            got(j, 12, 16)
            go(j, 16, 17)
        if tick == 0:
            arrive(halo.at[0], h_ssem.at[0], h_rsem.at[0])
            arrive(halo.at[1], h_ssem.at[1], h_rsem.at[1])
            normed[:TOK] = norm(halo.at[0])
            normed[2 * TOK :] = norm(halo.at[1])
        j = tick - 4
        if 0 <= j < CHUNKS:
            got(j, 16, 17)
            if j < QKV_CHUNKS:
                heads(j)

    state = tok_ref[...].astype(F32) + dot(att[...], wo[...].reshape(D, D))
    field = dot(rms_scale(state).astype(BF16), dec_ref[...]).astype(BF16)
    field = jnp.concatenate([field, jnp.zeros((TOK, TOK - V), BF16)], axis=1)

    row, col = iota((LANES, TOK), 0), iota((LANES, TOK), 1)
    lon = (4 * (row >> 4) - 2 + (row & 7)) & 63
    pick = hot(col == ((row >> 3) & 1) * 64 + lon)
    stage[...] = dot(pick, field).astype(BF16).reshape(MEMBERS, 16, TOK)
    for k in range(1, MEMBERS):
        send(stage.at[other(k)], recv.at[z], a_ssem.at[k], a_rsem.at[k], (other(k), p))
    recv[z] = stage[z]

    arrive(trec.at[0], t_ssem.at[0], t_rsem.at[0])
    arrive(trec.at[2], t_ssem.at[1], t_rsem.at[1])
    row, col = iota((LANES, 48), 0), iota((LANES, 48), 1)
    spot = (row & 7) + 2
    source = (spot >> 2) * 16 + ((row >> 3) & 1) * 4 + (spot & 3)
    truth_rows = dot(hot(col == source), trec[...].reshape(48, TOK)).astype(BF16)
    eye = hot(iota((VP, TOK), 0) == iota((VP, TOK), 1))
    truth_f = dot_t(eye, truth_rows)

    for k in range(1, MEMBERS):
        arrive(recv.at[other(MEMBERS - k)], a_ssem.at[k], a_rsem.at[k])
    fields = dot_t(eye, recv[...].reshape(LANES, TOK))

    def shifted(grid, k):
        return pltpu.roll(grid, (LANES - 16 * k) % LANES, axis=1)

    def row_sum(grid):
        return jnp.sum(grid * grid, axis=0, keepdims=True)

    e_all[1, 0:1] = row_sum(fields - truth_f)
    for k in range(1, MEMBERS // 2 + 1):
        e_k = row_sum(fields - shifted(fields, k))
        e_all[1, k : k + 1] = e_k
        if k < MEMBERS // 2:
            e_all[1, MEMBERS - k : MEMBERS - k + 1] = shifted(e_k, MEMBERS - k)

    send(e_all.at[1], e_all.at[0], e_ssem.at[0], e_rsem.at[0], high)
    send(e_all.at[1], e_all.at[2], e_ssem.at[1], e_rsem.at[1], low)
    arrive(e_all.at[0], e_ssem.at[0], e_rsem.at[0])
    arrive(e_all.at[2], e_ssem.at[1], e_rsem.at[1])

    lane = iota((MEMBERS, LANES), 1)
    north = ((lane >> 3) & 1) == 0
    below = jnp.where(p > 0, 1.0, 0.0)
    above = jnp.where(p < BANDS - 1, 1.0, 0.0)

    def swap(grid):
        return jnp.where(north, pltpu.roll(grid, LANES - 8, axis=1), pltpu.roll(grid, 8, axis=1))

    def along(grid):
        return pltpu.roll(grid, 1, axis=1) + grid + pltpu.roll(grid, LANES - 1, axis=1)

    e_low, e_own, e_high = e_all[0] * below, e_all[1], e_all[2] * above
    s_low, s_own, s_high = swap(e_low), swap(e_own), swap(e_high)
    box_own = along(e_own + s_own + jnp.where(north, s_low, s_high))
    box_out = along(s_own + jnp.where(north, e_high + s_high, e_low + s_low))
    d_own = jnp.sqrt(box_own / PATCH + EPS)
    d_out = jnp.sqrt(box_out / PATCH + EPS)
    first = iota((MEMBERS, LANES), 0) == 0
    scale = jnp.where(first, 1.0, 1.0 / (MEMBERS - 1))
    c_own = scale / d_own
    c_out = scale / d_out * jnp.where(north, above, below)
    btot = along(c_own + swap(c_own) + swap(c_out))

    part = jnp.sum(d_own * jnp.where(first, 1.0 / MEMBERS, -0.5 / (MEMBERS * (MEMBERS - 1))), axis=0, keepdims=True)
    for shift in (128, 64, 32, 16):
        part = part + pltpu.roll(part, shift, axis=1)
    score_ref[0:1] = part[:, 2:6]
    score_ref[1:2] = part[:, 10:14]

    grad = btot[0:1] * (fields - truth_f)
    for k in range(1, MEMBERS):
        grad = grad - btot[k : k + 1] * (fields - shifted(fields, k))
    grad = jnp.concatenate([grad, jnp.zeros((TOK - VP, LANES), F32)], axis=0)
    row, col = iota((TOK, LANES), 0), iota((TOK, LANES), 1)
    pick = hot(col == (row >> 3) * 16 + ((row >> 2) & 1) * 8 + 2 + (row & 3), F32)
    gsend[...] = dot_t(pick, grad, precision=lax.Precision.HIGHEST).reshape(MEMBERS, 8, TOK)
    for k in range(1, MEMBERS):
        send(gsend.at[other(k)], grecv.at[z], g_ssem.at[k], g_rsem.at[k], (other(k), p))
    grecv[z] = gsend[z]
    row, col = iota((TOK, TOK), 0), iota((TOK, TOK), 1)
    pick = hot(col == ((row & 63) >> 2) * 8 + (row >> 6) * 4 + (row & 3), F32)
    for k in range(1, MEMBERS):
        arrive(grecv.at[other(MEMBERS - k)], g_ssem.at[k], g_rsem.at[k])
    cells = dot(pick, grecv[...].reshape(TOK, TOK), precision=lax.Precision.HIGHEST)
    grad_ref[...] = cells.T[:V]
    for copy in sent:
        copy.wait_send()


def on_device(tokens, norm_gain, qkv_weight, out_weight, decode_weight, edges, truth):
    vmem = pl.BlockSpec(memory_space=pltpu.VMEM)
    dma = pltpu.SemaphoreType.DMA
    score, grad = pl.pallas_call(
        kernel,
        out_shape=(jax.ShapeDtypeStruct((2, 4), F32), jax.ShapeDtypeStruct((V, TOK), F32)),
        in_specs=[vmem] * 7,
        out_specs=(vmem, vmem),
        scratch_shapes=[
            pltpu.VMEM((QKV_CHUNKS, NX, NY, NC, 32, 3 * COLS), BF16),
            pltpu.VMEM((NX, NY, NC, 32, D), BF16),
            pltpu.VMEM((2, TOK, D), BF16),
            pltpu.VMEM((WIN, D), BF16),
            pltpu.VMEM((TOK, WIN), F32),
            pltpu.VMEM((TOK, D), BF16),
            pltpu.VMEM((MEMBERS, 16, TOK), BF16),
            pltpu.VMEM((MEMBERS, 16, TOK), BF16),
            pltpu.VMEM((3, 16, TOK), BF16),
            pltpu.VMEM((3, MEMBERS, LANES), F32),
            pltpu.VMEM((MEMBERS, 8, TOK), F32),
            pltpu.VMEM((MEMBERS, 8, TOK), F32),
            dma((CHUNKS, STEPS)),
            dma((CHUNKS, STEPS)),
            dma((2,)),
            dma((2,)),
            dma((2,)),
            dma((2,)),
            dma((MEMBERS,)),
            dma((MEMBERS,)),
            dma((2,)),
            dma((2,)),
            dma((MEMBERS,)),
            dma((MEMBERS,)),
        ],
        compiler_params=pltpu.CompilerParams(
            collective_id=0, has_side_effects=True, vmem_limit_bytes=48 * 1024 * 1024
        ),
    )(
        tokens.reshape(TOK, D),
        norm_gain.reshape(1, D),
        qkv_weight,
        out_weight,
        decode_weight,
        edges.reshape(TOK, FAN),
        truth.reshape(V, 8),
    )
    return score, grad.reshape(1, V, 2, 64)


def solution(mesh):
    in_specs = (
        P("member", "mp", None, None),
        P(),
        P("mp", None),
        P("mp", None),
        P(),
        P("mp", None, None),
        P(None, "mp", "member"),
    )
    out_specs = (P("mp", "member"), P("member", None, "mp", None))
    return jax.shard_map(on_device, mesh=mesh, in_specs=in_specs, out_specs=out_specs, check_vma=False)
```

time: 253 us -> 79.3 us (0.31)
  the two profiles are of different devices: /device:TPU:6 before, /device:TPU:1 now
where the time goes in v1:
time: 79.3 us; the launch traced here: 78.5 us
  Pallas kernels  74.5 us (94%)
  local copies, waits for them, and re-layouts  3.35 us (4%)
    pallas_call x1, Pallas kernels, on_device(): pl.pallas_call(kernel, out_shape=(jax.ShapeDtypeStruct((2, 4), F32), jax....  74.5 us
    unnamed x13, local copies, waits for them, and re-layouts  1.81 us

profile of v1, /device:TPU:1, one launch (start us, length us, event | category | flops | bytes accessed | tf_op | source)
XLA Modules:
  0.0 78.5 jit_solution(7855452808930426189)
XLA Ops:
  0.6 0.0 copy-start.4
  0.6 0.8 %copy.15.truth_ref = bf16[90,8]{1,0:T(8,128)(2,1)S(1)} copy(bf16[90,8]{0,1:T(8,128)(2,1)} %bitcast.9) | data formatting | bytes 2880 | tf_op jit(solution)/shard_map/reshape | solution.py:349
  1.4 0.0 copy-done.4
  1.4 0.0 copy-start
  1.5 0.1 copy.13
  1.5 0.0 copy-start.1
  1.5 0.0 copy-start.2
  1.5 0.0 copy-start.3
  1.6 1.1 %copy.14.dec_ref = bf16[1024,90]{1,0:T(8,128)(2,1)S(1)} copy(bf16[1024,90]{0,1:T(8,128)(2,1)} %param.11) | data formatting | bytes 368640 | tf_op args[4]
  2.7 0.0 copy-done
  2.7 0.0 copy-done.1
  2.7 0.0 copy-done.2
  2.7 0.0 copy-done.3
  2.7 74.5 %shard_map.86 = (f32[2,4]{1,0:T(2,128)S(1)}, f32[90,128]{1,0:T(8,128)S(1)}) custom-call(bf16[128,1024]{1,0:T(8,128)(2,1)S(1)} %bitcast.5, f32[1,1024]{1,0:T(1,128)S(1)} %bitcast.7, bf16[32,3072]{1,0:T(8,128)(2,1)S(1)} %copy-done.1, bf16[32,1024]{1,0:T(8,128)(2,1)S(1)} %copy-done.2, bf16[1024,90]{1,0:T(8,128)(2,1)S(1)} %copy.14.dec_ref, ...), custom_call_target="tpu_custom_call" | custom-call | tf_op jit(solution)/shard_map/pallas_call | solution.py:308
  77.2 0.7 copy.16
  78.0 0.6 copy.18
Async XLA Ops:
  0.6 0.8 %copy-start.4 = (s32[2,64,16]{1,2,0:T(8,128)S(1)}, s32[2,64,16]{1,2,0:T(8,128)}, u32[]{:S(2)}) copy-start(s32[2,64,16]{1,2,0:T(8,128)} %param.12) | copy-start | bytes 24580
  1.4 1.3 %copy-start = (bf16[1,2,64,1024]{3,2,1,0:T(8,128)(2,1)S(1)}, bf16[1,2,64,1024]{3,2,1,0:T(8,128)(2,1)}, u32[]{:S(2)}) copy-start(bf16[1,2,64,1024]{3,2,1,0:T(8,128)(2,1)} %param.7) | copy-start | bytes 786436
  1.5 1.2 %copy-start.1 = (bf16[32,3072]{1,0:T(8,128)(2,1)S(1)}, bf16[32,3072]{1,0:T(8,128)(2,1)}, u32[]{:S(2)}) copy-start(bf16[32,3072]{1,0:T(8,128)(2,1)} %wqkv_ref.1) | copy-start | bytes 589828
  1.5 1.2 %copy-start.2 = (bf16[32,1024]{1,0:T(8,128)(2,1)S(1)}, bf16[32,1024]{1,0:T(8,128)(2,1)}, u32[]{:S(2)}) copy-start(bf16[32,1024]{1,0:T(8,128)(2,1)} %wout_ref.1) | copy-start | bytes 196612
  1.5 1.2 %copy-start.3 = (f32[1024]{0:T(1024)S(1)}, f32[1024]{0:T(1024)}, u32[]{:S(2)}) copy-start(f32[1024]{0:T(1024)} %param.8) | copy-start | bytes 12292

commit v2 on v1

v2 whole, which is shorter than its diff:
```python
import jax
import jax.numpy as jnp
from jax import lax
from jax.experimental import pallas as pl
from jax.experimental.pallas import tpu as pltpu
from jax.sharding import PartitionSpec as P

MESH = pl.DeviceIdType.MESH
F32, BF16 = jnp.float32, jnp.bfloat16
EPS = 1e-05
NX, NY, NC = 4, 4, 2
MEMBERS = 16
BANDS = NX * NY * NC
TOK = 128
WIN = 3 * TOK
D = 1024
V = 90
VP = 96
FAN = 16
HEADS_C = 4
QKV_CHUNKS = 4
OUT_CHUNKS = 2
CHUNKS = QKV_CHUNKS + OUT_CHUNKS
COLS = 256
OUT_COLS = D // OUT_CHUNKS
STEPS = 33
REACH = 4
HALF = VP // 2
TILE = MEMBERS * 16
PATCH = 9.0 * V
FAR_FIRST, FAR_SECOND = (0,), (CHUNKS - 1,)
PAIRS = {0: 1}
ORDER = (
    ("first", 0), ("relay", 2), ("halo", 0), ("relay", 3), ("relay", 4), ("relay", 5), ("second", 2), ("again", 0),
    ("second", 3), ("core", 0), ("again", 2), ("second", 4), ("truth", 0), ("done", 0), ("heads", 0), ("again", 3),
    ("core", 2), ("second", 5), ("core", 1), ("done", 2), ("heads", 2), ("again", 4), ("core", 3), ("done", 1),
    ("heads", 1), ("core", 4), ("core", 5), ("done", 3), ("heads", 3), ("done", 4), ("out", 4), ("done", 5),
    ("out", 5),
)


def iota(shape, dim):
    return lax.broadcasted_iota(jnp.int32, shape, dim)


def hot(mask, dtype=BF16):
    return jnp.where(mask, 1.0, 0.0).astype(dtype)


def dot(a, b, **kw):
    return jnp.dot(a, b, preferred_element_type=F32, **kw)


def dot_t(a, b, **kw):
    return lax.dot_general(a, b, (((1,), (1,)), ((), ())), preferred_element_type=F32, **kw)


def rms_scale(v):
    return v * lax.rsqrt(jnp.mean(v * v, axis=-1, keepdims=True) + EPS)


def kernel(
    tok_hbm, gain_hbm, wqkv_hbm, wout_hbm, dec_hbm, edge_hbm, truth_hbm,
    score_ref, grad_ref,
    tok_ref, gain_ref, dec_ref, edge_ref, truth_ref, wq, wo, halo, normed, count, att, state, dec, truths, fields, pick, e_all,
    in_sem, w_ssem, w_rsem, h_ssem, h_rsem, t_ssem, t_rsem, f_ssem, f_rsem, e_ssem, e_rsem,
):
    z = lax.axis_index("member")
    p = lax.axis_index("mp")
    x, y, c = lax.div(p, NY * NC), lax.rem(lax.div(p, NC), NY), lax.rem(p, NC)
    xm, xp, x2 = lax.rem(x + 3, NX), lax.rem(x + 1, NX), lax.rem(x + 2, NX)
    ym, yp, y2 = lax.rem(y + 3, NY), lax.rem(y + 1, NY), lax.rem(y + 2, NY)

    def chip(cx, cy, cc):
        return (z, (cx * NY + cy) * NC + cc)

    odd = lax.rem(z, 2)

    def columns(j, size):
        first = QKV_CHUNKS if j >= QKV_CHUNKS else 0
        if j in PAIRS:
            return pl.multiple_of((j - first + odd) * size, size)
        if j in PAIRS.values():
            return pl.multiple_of((j - first - odd) * size, size)
        return (j - first) * size

    at_xp, at_xm, at_yp, at_ym = chip(xp, y, c), chip(xm, y, c), chip(x, yp, c), chip(x, ym, c)
    at_x2, at_y2 = chip(x2, y, c), chip(x, y2, c)
    sib = chip(x, y, 1 - c)
    low, high = (z, lax.rem(p + BANDS - 1, BANDS)), (z, lax.rem(p + 1, BANDS))

    def other(k):
        return lax.rem(z + (k + MEMBERS), MEMBERS)

    barrier = pltpu.get_barrier_semaphore()
    partners = [at_xp, at_xm, at_yp, at_ym, at_x2, at_y2, sib, low, high]
    partners += [(other(k), p) for k in range(-REACH, REACH + 1) if k]
    for target in partners:
        pl.semaphore_signal(barrier, inc=1, device_id=target, device_id_type=MESH)

    loads = []

    def load(src, dst):
        copy = pltpu.make_async_copy(src, dst, in_sem.at[len(loads)])
        copy.start()
        loads.append(copy)

    gathered = [j for j in range(CHUNKS) if j not in PAIRS.values()]
    for j in gathered:
        if j < QKV_CHUNKS:
            for part in range(3):
                load(
                    wqkv_hbm.at[:, pl.ds(part * D + columns(j, COLS), COLS)],
                    wq.at[j, x, y, c, :, pl.ds(part * COLS, COLS)],
                )
        else:
            load(wout_hbm.at[:, pl.ds(columns(j, OUT_COLS), OUT_COLS)], wo.at[j - QKV_CHUNKS, x, y, c])
    weight_loads = len(loads)
    small = ((truth_hbm, truth_ref), (gain_hbm, gain_ref), (edge_hbm, edge_ref), (dec_hbm, dec_ref))
    for src, dst in ((tok_hbm, tok_ref),) + small:
        load(src, dst)
    for copy in loads[: weight_loads + 2]:
        copy.wait()
    cells = jnp.concatenate([truth_ref[0], truth_ref[1], jnp.zeros((8, V), BF16)], axis=0)
    truths[z] = jnp.concatenate([cells, jnp.zeros((16, TOK - V), BF16)], axis=1)
    pl.semaphore_wait(barrier, len(partners))

    sent = []

    def send(src, dst, ssem, rsem, target):
        copy = pltpu.make_async_remote_copy(
            src_ref=src, dst_ref=dst, send_sem=ssem, recv_sem=rsem, device_id=target, device_id_type=MESH
        )
        copy.start()
        sent.append(copy)

    def arrive(dst, ssem, rsem):
        pltpu.make_async_remote_copy(
            src_ref=dst, dst_ref=dst, send_sem=ssem, recv_sem=rsem, device_id=sib, device_id_type=MESH
        ).wait_recv()

    def buf(j):
        return (wq.at[j], 3 * COLS) if j < QKV_CHUNKS else (wo.at[j - QKV_CHUNKS], OUT_COLS)

    A, B = pl.ds(0, 16), pl.ds(16, 16)
    ALL = slice(None)

    def pieces(j, step):
        _, n = buf(j)
        lo, hi = pl.ds(0, n // 2), pl.ds(n // 2, n // 2)
        if step == "start":
            near = [
                (0, (x, y, c, A), at_xp, (xm, y, c, A)),
                (1, (x, y, c, A), at_xm, (xp, y, c, A)),
                (2, (x, y, c, B), at_yp, (x, ym, c, B)),
                (3, (x, y, c, B), at_ym, (x, yp, c, B)),
            ]
            far = [(4, (x, y, c, A), at_x2, (x2, y, c, A)), (6, (x, y, c, B), at_y2, (x, y2, c, B))]
            return near + far if j in FAR_FIRST else near
        if step == "relay":
            return [
                (4, (xm, y, c, A, lo), at_xp, (x2, y, c, A, lo)),
                (5, (xp, y, c, A, hi), at_xm, (x2, y, c, A, hi)),
                (6, (x, ym, c, B, lo), at_yp, (x, y2, c, B, lo)),
                (7, (x, yp, c, B, hi), at_ym, (x, y2, c, B, hi)),
            ]
        if step == "second":
            near = [
                (8, (ALL, y, c, A), at_yp, (ALL, ym, c, A)),
                (9, (ALL, y, c, A), at_ym, (ALL, yp, c, A)),
                (10, (x, ALL, c, B), at_xp, (xm, ALL, c, B)),
                (11, (x, ALL, c, B), at_xm, (xp, ALL, c, B)),
            ]
            far = [(12, (ALL, y, c, A), at_y2, (ALL, y2, c, A)), (14, (x, ALL, c, B), at_x2, (x2, ALL, c, B))]
            return far + near if j in FAR_SECOND else near
        if step == "again":
            return [
                (12, (ALL, ym, c, A, lo), at_yp, (ALL, y2, c, A, lo)),
                (13, (ALL, yp, c, A, hi), at_ym, (ALL, y2, c, A, hi)),
                (14, (xm, ALL, c, B, lo), at_xp, (x2, ALL, c, B, lo)),
                (15, (xp, ALL, c, B, hi), at_xm, (x2, ALL, c, B, hi)),
            ]
        if step == "core_near":
            return [(16, (ALL, y, c, A), sib, (ALL, y, 1 - c, A)), (17, (x, ALL, c, B), sib, (x, ALL, 1 - c, B))]
        if step == "core_next":
            return [
                (18, (ALL, ym, c, A), sib, (ALL, ym, 1 - c, A)),
                (19, (ALL, yp, c, A), sib, (ALL, yp, 1 - c, A)),
                (20, (xm, ALL, c, B), sib, (xm, ALL, 1 - c, B)),
                (21, (xp, ALL, c, B), sib, (xp, ALL, 1 - c, B)),
            ]
        return [(22, (ALL, y2, c, A), sib, (ALL, y2, 1 - c, A)), (23, (x2, ALL, c, B), sib, (x2, ALL, 1 - c, B))]

    def go(j, step):
        ref, _ = buf(j)
        for i, src, target, _ in pieces(j, step):
            send(ref.at[src], ref.at[src], w_ssem.at[j, i], w_rsem.at[j, i], target)

    def got(j, *steps):
        ref, _ = buf(j)
        for step in steps:
            for i, _, _, dst in pieces(j, step):
                arrive(ref.at[dst], w_ssem.at[j, i], w_rsem.at[j, i])

    up, down = (other(1), p), (other(-1), p)
    Z_NEAR = [
        (24, (ALL, ym, c, A), up), (25, (ALL, y, c, A), up), (26, (ALL, yp, c, A), up),
        (27, (xm, ALL, c, B), down), (28, (x, ALL, c, B), down), (29, (xp, ALL, c, B), down),
    ]
    Z_LAST = [(30, (ALL, y2, c, A), up), (31, (x2, ALL, c, B), down)]

    def go_z(j, part):
        if j in PAIRS:
            mine, theirs, k = buf(j)[0], buf(PAIRS[j])[0], PAIRS[j]
            for i, where, target in part:
                send(mine.at[where], theirs.at[where], w_ssem.at[k, i], w_rsem.at[k, i], target)

    def reach(ref, ssem, rsem):
        for d in range(REACH, 0, -1):
            send(ref.at[z], ref.at[z], ssem.at[d], rsem.at[d], (other(d), p))
            send(ref.at[z], ref.at[z], ssem.at[REACH + d], rsem.at[REACH + d], (other(-d), p))

    def relay(ref, ssem, rsem):
        behind, ahead = ref.at[other(-REACH)], ref.at[other(REACH)]
        arrive(behind, ssem.at[REACH], rsem.at[REACH])
        arrive(ahead, ssem.at[2 * REACH], rsem.at[2 * REACH])
        rows = ref.shape[1] // 2
        if rows % 16 == 0:
            first, second = pl.ds(0, rows), pl.ds(rows, rows)
            send(behind.at[first], behind.at[first], ssem.at[12], rsem.at[12], (other(REACH), p))
            send(ahead.at[second], ahead.at[second], ssem.at[16], rsem.at[16], (other(-REACH), p))
        else:
            send(behind, behind, ssem.at[12], rsem.at[12], (other(REACH), p))
        for d in range(REACH - 1, 0, -1):
            send(behind, behind, ssem.at[8 + d], rsem.at[8 + d], (other(d), p))
            send(ahead, ahead, ssem.at[12 + d], rsem.at[12 + d], (other(-d), p))

    def reached(ref, ssem, rsem):
        for d in range(1, REACH):
            arrive(ref.at[other(-d)], ssem.at[d], rsem.at[d])
            arrive(ref.at[other(d)], ssem.at[REACH + d], rsem.at[REACH + d])
        for d in range(1, REACH):
            arrive(ref.at[other(-REACH - d)], ssem.at[8 + d], rsem.at[8 + d])
            arrive(ref.at[other(REACH + d)], ssem.at[12 + d], rsem.at[12 + d])
        opposite = ref.at[other(MEMBERS // 2)]
        rows = ref.shape[1] // 2
        if rows % 16 == 0:
            arrive(opposite.at[pl.ds(0, rows)], ssem.at[12], rsem.at[12])
            arrive(opposite.at[pl.ds(rows, rows)], ssem.at[16], rsem.at[16])
        else:
            arrive(opposite, ssem.at[12], rsem.at[12])

    go(0, "start")
    for j in gathered[1:]:
        go(j, "start")
    reach(truths, t_ssem, t_rsem)

    def norm(rows):
        return (rms_scale(rows[...].astype(F32)) * gain_ref[...]).astype(BF16)

    for copy in loads[weight_loads + 2 :]:
        copy.wait()
    normed[TOK : 2 * TOK] = norm(tok_ref)
    local = jnp.concatenate([edge_ref[0], edge_ref[1]], axis=1) - (p - 1) * TOK
    nodes = iota((WIN, TOK), 0)
    total = jnp.zeros((WIN, TOK), F32)
    for k in range(FAN):
        total += jnp.where(local[k : k + 1] == nodes, 1.0, 0.0)
    count[...] = total.T
    dec[...] = jnp.zeros_like(dec)
    dec[:V] = dec_ref[...]
    row, col = iota((MEMBERS * TOK, TILE), 0), iota((MEMBERS * TOK, TILE), 1)
    cell = ((col >> 3) & 1) * 64 + ((4 * z - 2 + (col & 7)) & 63)
    pick[...] = hot(row == (col >> 4) * TOK + cell)

    def heads(j):
        weight = wq[j].reshape(D, 3 * COLS)
        query = dot(normed[TOK : 2 * TOK], weight[:, :COLS]).astype(BF16)
        keyval = dot(normed[...], weight[:, COLS:]).astype(BF16)
        key, value = keyval[:, :COLS], keyval[:, COLS:]
        head_of = iota((TOK, COLS), 1) >> 6
        spread = jnp.concatenate(
            [jnp.where(head_of == h, query, jnp.zeros_like(query)) for h in range(HEADS_C)], axis=0
        )
        scores = dot_t(spread, key) * 0.125
        times = count[...]
        probs = []
        for h in range(HEADS_C):
            s = jnp.where(times > 0.0, scores[h * TOK : (h + 1) * TOK], -1e30)
            expo = jnp.exp(s - jnp.max(s, axis=-1, keepdims=True)) * times
            probs.append((expo * (1.0 / jnp.sum(expo, axis=-1, keepdims=True))).astype(BF16))
        mixed = dot(jnp.concatenate(probs, axis=0), value)
        out = jnp.zeros((TOK, COLS), F32)
        for h in range(HEADS_C):
            out = jnp.where(head_of == h, mixed[h * TOK : (h + 1) * TOK], out)
        att[:, pl.ds(columns(j, COLS), COLS)] = out.astype(BF16)

    def project(j):
        i = j - QKV_CHUNKS
        where = pl.ds(columns(j, OUT_COLS), OUT_COLS)
        state[:, where] = tok_ref[:, where].astype(F32) + dot(att[...], wo[i].reshape(D, OUT_COLS))

    for step, j in ORDER:
        if step == "halo":
            send(tok_ref, halo.at[1], h_ssem.at[1], h_rsem.at[1], low)
            send(tok_ref, halo.at[0], h_ssem.at[0], h_rsem.at[0], high)
            continue
        if step == "truth":
            relay(truths, t_ssem, t_rsem)
            continue
        if step == "first":
            got(j, "start")
            go(j, "second")
            go(j, "core_near")
        elif step == "relay":
            got(j, "start")
            go(j, "relay")
        elif step == "second":
            got(j, "relay")
            go(j, "second")
            go(j, "core_near")
        elif step == "again":
            got(j, "second")
            go_z(j, Z_NEAR)
            go(j, "again")
            go(j, "core_next")
        elif step == "core" and j in PAIRS.values():
            ref = buf(j)[0]
            for i, where, _ in Z_NEAR + Z_LAST:
                arrive(ref.at[where], w_ssem.at[j, i], w_rsem.at[j, i])
            send(ref.at[ALL, ALL, c], ref.at[ALL, ALL, c], w_ssem.at[j, 32], w_rsem.at[j, 32], sib)
        elif step == "core":
            if j in FAR_SECOND:
                got(j, "second")
                go(j, "core_next")
            else:
                got(j, "again")
            go_z(j, Z_LAST)
            go(j, "core_last")
        elif step == "done" and j in PAIRS.values():
            arrive(buf(j)[0].at[ALL, ALL, 1 - c], w_ssem.at[j, 32], w_rsem.at[j, 32])
        elif step == "done":
            got(j, "core_near", "core_next", "core_last")
        elif step == "out":
            project(j)
        elif step == "heads":
            if j == 0:
                arrive(halo.at[0], h_ssem.at[0], h_rsem.at[0])
                arrive(halo.at[1], h_ssem.at[1], h_rsem.at[1])
                normed[:TOK] = norm(halo.at[0])
                normed[2 * TOK :] = norm(halo.at[1])
            heads(j)

    fields[z] = dot_t(dec[...], rms_scale(state[...]).astype(BF16)).astype(BF16)
    reach(fields, f_ssem, f_rsem)

    reached(truths, t_ssem, t_rsem)
    row, col = iota((TOK, TILE), 0), iota((TOK, TILE), 1)
    source = ((row & 63) >> 2) * 16 + (row >> 6) * 4 + (row & 3)
    truth_rows = dot(hot(col == source), truths[...].reshape(TILE, TOK)).astype(BF16)
    eye = hot(iota((VP, TOK), 0) == iota((VP, TOK), 1))
    truth_b = dot_t(eye, truth_rows)
    spot = ((col >> 3) & 1) * 64 + ((4 * z - 2 + (col & 7)) & 63)
    truth_tile = dot(truth_b.astype(BF16), hot(row == spot))
    own = fields[z].astype(F32)

    relay(fields, f_ssem, f_rsem)
    reached(fields, f_ssem, f_rsem)

    def row_sum(grid):
        return jnp.sum(grid * grid, axis=0, keepdims=True)

    e_all[1, 0:1, :TOK] = row_sum(own - truth_b)
    for k in range(1, MEMBERS):
        e_all[1, k : k + 1, :TOK] = row_sum(own - fields[other(k)].astype(F32))
    tile = dot(jnp.concatenate([fields[m] for m in range(MEMBERS)], axis=1), pick[...])
    e_all[1, 8:16, TOK:] = jnp.zeros((8, TILE), F32)
    e_all[1, 0:1, TOK:] = row_sum(tile - truth_tile)
    for k in range(1, MEMBERS // 2 + 1):
        e_all[1, k : k + 1, TOK:] = row_sum(tile - pltpu.roll(tile, TILE - 16 * k, axis=1))

    send(e_all.at[1], e_all.at[0], e_ssem.at[0], e_rsem.at[0], high)
    send(e_all.at[1], e_all.at[2], e_ssem.at[1], e_rsem.at[1], low)
    arrive(e_all.at[0], e_ssem.at[0], e_rsem.at[0])
    arrive(e_all.at[2], e_ssem.at[1], e_rsem.at[1])

    below = jnp.where(p > 0, 1.0, 0.0)
    above = jnp.where(p < BANDS - 1, 1.0, 0.0)
    e_low, e_own, e_high = e_all[0] * below, e_all[1], e_all[2] * above

    lane = iota((MEMBERS, TOK), 1)
    north, lon = lane < 64, lane & 63

    def swap(grid):
        return pltpu.roll(grid, 64, axis=1)

    def along(grid):
        west = jnp.where(lon == 0, pltpu.roll(grid, 65, axis=1), pltpu.roll(grid, 1, axis=1))
        east = jnp.where(lon == 63, pltpu.roll(grid, 63, axis=1), pltpu.roll(grid, TOK - 1, axis=1))
        return west + grid + east

    r_low, r_own, r_high = e_low[:, :TOK], e_own[:, :TOK], e_high[:, :TOK]
    s_low, s_own, s_high = swap(r_low), swap(r_own), swap(r_high)
    box_own = along(r_own + s_own + jnp.where(north, s_low, s_high))
    box_out = along(s_own + jnp.where(north, r_high + s_high, r_low + s_low))
    scale = jnp.where(iota((MEMBERS, TOK), 0) == 0, 1.0, 1.0 / (MEMBERS - 1))
    c_own = scale / jnp.sqrt(box_own / PATCH + EPS)
    c_out = scale / jnp.sqrt(box_out / PATCH + EPS) * jnp.where(north, above, below)
    btot = along(c_own + swap(c_own) + swap(c_out))
    grad = btot[0:1] * (own - truth_b)
    for k in range(1, MEMBERS):
        grad = grad - btot[k : k + 1] * (own - fields[other(k)].astype(F32))
    grad_ref[...] = grad[:V]

    lane = iota((MEMBERS, TILE), 1)
    north = ((lane >> 3) & 1) == 0

    def swap_tile(grid):
        return jnp.where(north, pltpu.roll(grid, TILE - 8, axis=1), pltpu.roll(grid, 8, axis=1))

    t_own = e_own[:, TOK:]
    rows = t_own + swap_tile(t_own) + jnp.where(north, swap_tile(e_low[:, TOK:]), swap_tile(e_high[:, TOK:]))
    box = pltpu.roll(rows, 1, axis=1) + rows + pltpu.roll(rows, TILE - 1, axis=1)
    apart = iota((MEMBERS, TILE), 0)
    pair = 0.5 / (MEMBERS * (MEMBERS - 1))
    weight = jnp.where(apart == 0, 1.0 / MEMBERS, jnp.where(apart < MEMBERS // 2, -2.0 * pair, -pair))
    weight = jnp.where(apart > MEMBERS // 2, 0.0, weight)
    part = jnp.sum(jnp.sqrt(box / PATCH + EPS) * weight, axis=0, keepdims=True)
    for shift in (128, 64, 32, 16):
        part = part + pltpu.roll(part, shift, axis=1)
    score_ref[0:1] = part[:, 2:6]
    score_ref[1:2] = part[:, 10:14]
    for copy in sent:
        copy.wait_send()


def on_device(tokens, norm_gain, qkv_weight, out_weight, decode_weight, edges, truth):
    vmem = pl.BlockSpec(memory_space=pltpu.VMEM)
    dma = pltpu.SemaphoreType.DMA
    score, grad = pl.pallas_call(
        kernel,
        out_shape=(jax.ShapeDtypeStruct((2, 4), F32), jax.ShapeDtypeStruct((V, TOK), F32)),
        in_specs=[pl.BlockSpec(memory_space=pltpu.HBM)] * 7,
        out_specs=(vmem, vmem),
        scratch_shapes=[
            pltpu.VMEM((TOK, D), BF16),
            pltpu.VMEM((1, D), F32),
            pltpu.VMEM((V, D), BF16),
            pltpu.VMEM((2, FAN, 64), jnp.int32),
            pltpu.VMEM((2, 4, V), BF16),
            pltpu.VMEM((QKV_CHUNKS, NX, NY, NC, 32, 3 * COLS), BF16),
            pltpu.VMEM((OUT_CHUNKS, NX, NY, NC, 32, OUT_COLS), BF16),
            pltpu.VMEM((2, TOK, D), BF16),
            pltpu.VMEM((WIN, D), BF16),
            pltpu.VMEM((TOK, WIN), F32),
            pltpu.VMEM((TOK, D), BF16),
            pltpu.VMEM((TOK, D), F32),
            pltpu.VMEM((VP, D), BF16),
            pltpu.VMEM((MEMBERS, 16, TOK), BF16),
            pltpu.VMEM((MEMBERS, VP, TOK), BF16),
            pltpu.VMEM((MEMBERS * TOK, TILE), BF16),
            pltpu.VMEM((3, MEMBERS, TOK + TILE), F32),
            dma((3 * QKV_CHUNKS + OUT_CHUNKS + 5,)),
            dma((CHUNKS, STEPS)),
            dma((CHUNKS, STEPS)),
            dma((2,)),
            dma((2,)),
            dma((4 * REACH + 1,)),
            dma((4 * REACH + 1,)),
            dma((4 * REACH + 1,)),
            dma((4 * REACH + 1,)),
            dma((2,)),
            dma((2,)),
        ],
        compiler_params=pltpu.CompilerParams(
            collective_id=0, has_side_effects=True, vmem_limit_bytes=48 * 1024 * 1024
        ),
    )(
        *(pltpu.with_memory_space_constraint(a, pltpu.HBM) for a in (
            tokens.reshape(TOK, D),
            norm_gain.reshape(1, D),
            qkv_weight,
            out_weight,
            decode_weight.T,
            edges.transpose(0, 2, 1),
            truth.transpose(1, 2, 0),
        ))
    )
    return score, grad.reshape(1, V, 2, 64)


def solution(mesh):
    in_specs = (
        P("member", "mp", None, None),
        P(),
        P("mp", None),
        P("mp", None),
        P(),
        P("mp", None, None),
        P(None, "mp", "member"),
    )
    out_specs = (P("mp", "member"), P("member", None, "mp", None))
    return jax.shard_map(on_device, mesh=mesh, in_specs=in_specs, out_specs=out_specs, check_vma=False)
```

time: 79.3 us -> 67.7 us (0.85)
  Pallas kernels: 74.5 us -> 65.7 us
  local copies, waits for them, and re-layouts: 3.35 us -> 1.29 us
    pallas_call x1, Pallas kernels: 74.5 us -> 65.7 us  [on_device(): pl.pallas_call(kernel, out_shape=(jax.ShapeDtypeStruct((2, 4), F32), jax....]
    unnamed x13 -> x1, local copies, waits for them, and re-layouts: 1.81 us -> 0.56 us
    reshape x1 -> x0, local copies, waits for them, and re-layouts: 0.8 us -> none  [on_device(): truth.reshape(V, 8)]
where the time goes in v2:
time: 67.7 us; the launch traced here: 67.6 us
  Pallas kernels  65.7 us (97%)
  local copies, waits for them, and re-layouts  1.29 us (2%)
    pallas_call x1, Pallas kernels, on_device(): pl.pallas_call(kernel, out_shape=(jax.ShapeDtypeStruct((2, 4), F32), jax....  65.7 us

profile of v2, /device:TPU:1, one launch (start us, length us, event | category | flops | bytes accessed | tf_op | source)
XLA Modules:
  0.0 67.6 jit_solution(17079898602733609464)
XLA Ops:
  0.6 65.7 %shard_map.86 = (f32[2,4]{1,0:T(2,128)S(1)}, f32[90,128]{1,0:T(8,128)S(1)}) custom-call(bf16[128,1024]{1,0:T(8,128)(2,1)} %bitcast.6, f32[1,1024]{1,0:T(1,128)} %bitcast.10, bf16[32,3072]{1,0:T(8,128)(2,1)} %wqkv_hbm.1, bf16[32,1024]{1,0:T(8,128)(2,1)} %wout_hbm.1, bf16[90,1024]{1,0:T(8,128)(2,1)} %bitcast.7, s32[2,16,64]{2,1,0:T(8,128)} %bitcast.9, ...), custom_call_target="tpu_custom_call" | custom-call | tf_op jit(solution)/shard_map/pallas_call | solution.py:440
  66.3 0.7 %copy.10 = f32[90,128]{0,1:T(8,128)} copy(f32[90,128]{1,0:T(8,128)S(1)} %get-tuple-element.5) | data formatting | bytes 92160 | tf_op jit(solution)/shard_map/pallas_call | solution.py:440
  67.0 0.6 copy.12

commit v3 on v2

--- a/solution.py
+++ b/solution.py
@@ -28,14 +28,13 @@
 HALF = VP // 2
 TILE = MEMBERS * 16
 PATCH = 9.0 * V
-FAR_FIRST, FAR_SECOND = (0,), (CHUNKS - 1,)
+FAR_FIRST, FAR_SECOND = (0, 2, 3), (CHUNKS - 1,)
 PAIRS = {0: 1}
 ORDER = (
-    ("first", 0), ("relay", 2), ("halo", 0), ("relay", 3), ("relay", 4), ("relay", 5), ("second", 2), ("again", 0),
-    ("second", 3), ("core", 0), ("again", 2), ("second", 4), ("truth", 0), ("done", 0), ("heads", 0), ("again", 3),
-    ("core", 2), ("second", 5), ("core", 1), ("done", 2), ("heads", 2), ("again", 4), ("core", 3), ("done", 1),
-    ("heads", 1), ("core", 4), ("core", 5), ("done", 3), ("heads", 3), ("done", 4), ("out", 4), ("done", 5),
-    ("out", 5),
+    ("first", 0), ("first", 2), ("first", 3), ("relay", 4), ("relay", 5), ("again", 0), ("halo", 0), ("again", 2),
+    ("core", 0), ("second", 4), ("again", 3), ("second", 5), ("core", 2), ("truth", 0), ("done", 0), ("heads", 0),
+    ("core", 1), ("again", 4), ("core", 3), ("done", 2), ("heads", 2), ("done", 1), ("heads", 1), ("core", 4),
+    ("core", 5), ("done", 3), ("heads", 3), ("done", 4), ("out", 4), ("done", 5), ("out", 5),
 )
 
 
@@ -235,10 +234,12 @@
             send(behind, behind, ssem.at[8 + d], rsem.at[8 + d], (other(d), p))
             send(ahead, ahead, ssem.at[12 + d], rsem.at[12 + d], (other(-d), p))
 
-    def reached(ref, ssem, rsem):
+    def reached_near(ref, ssem, rsem):
         for d in range(1, REACH):
             arrive(ref.at[other(-d)], ssem.at[d], rsem.at[d])
             arrive(ref.at[other(d)], ssem.at[REACH + d], rsem.at[REACH + d])
+
+    def reached_far(ref, ssem, rsem):
         for d in range(1, REACH):
             arrive(ref.at[other(-REACH - d)], ssem.at[8 + d], rsem.at[8 + d])
             arrive(ref.at[other(REACH + d)], ssem.at[12 + d], rsem.at[12 + d])
@@ -352,9 +353,13 @@
             heads(j)
 
     fields[z] = dot_t(dec[...], rms_scale(state[...]).astype(BF16)).astype(BF16)
+    before = len(sent)
     reach(fields, f_ssem, f_rsem)
-
-    reached(truths, t_ssem, t_rsem)
+    for copy in sent[:before]:
+        copy.wait_send()
+
+    reached_near(truths, t_ssem, t_rsem)
+    reached_far(truths, t_ssem, t_rsem)
     row, col = iota((TOK, TILE), 0), iota((TOK, TILE), 1)
     source = ((row & 63) >> 2) * 16 + (row >> 6) * 4 + (row & 3)
     truth_rows = dot(hot(col == source), truths[...].reshape(TILE, TOK)).astype(BF16)
@@ -364,17 +369,23 @@
     truth_tile = dot(truth_b.astype(BF16), hot(row == spot))
     own = fields[z].astype(F32)
 
-    relay(fields, f_ssem, f_rsem)
-    reached(fields, f_ssem, f_rsem)
-
     def row_sum(grid):
         return jnp.sum(grid * grid, axis=0, keepdims=True)
 
+    def own_row(k):
+        e_all[1, k : k + 1, :TOK] = row_sum(own - fields[other(k)].astype(F32))
+
     e_all[1, 0:1, :TOK] = row_sum(own - truth_b)
-    for k in range(1, MEMBERS):
-        e_all[1, k : k + 1, :TOK] = row_sum(own - fields[other(k)].astype(F32))
+    e_all[1, 8:16, TOK:] = jnp.zeros((8, TILE), F32)
+    relay(fields, f_ssem, f_rsem)
+    reached_near(fields, f_ssem, f_rsem)
+    for k in range(1, REACH + 1):
+        own_row(k)
+        own_row(MEMBERS - k)
+    reached_far(fields, f_ssem, f_rsem)
+    for k in range(REACH + 1, MEMBERS - REACH):
+        own_row(k)
     tile = dot(jnp.concatenate([fields[m] for m in range(MEMBERS)], axis=1), pick[...])
-    e_all[1, 8:16, TOK:] = jnp.zeros((8, TILE), F32)
     e_all[1, 0:1, TOK:] = row_sum(tile - truth_tile)
     for k in range(1, MEMBERS // 2 + 1):
         e_all[1, k : k + 1, TOK:] = row_sum(tile - pltpu.roll(tile, TILE - 16 * k, axis=1))
@@ -430,7 +441,7 @@
         part = part + pltpu.roll(part, shift, axis=1)
     score_ref[0:1] = part[:, 2:6]
     score_ref[1:2] = part[:, 10:14]
-    for copy in sent:
+    for copy in sent[before:]:
         copy.wait_send()
 
 

time: 67.7 us -> 65.2 us (0.963)
  Pallas kernels: 65.7 us -> 63.2 us
    pallas_call x1, Pallas kernels: 65.7 us -> 63.2 us  [on_device(): pl.pallas_call(kernel, out_shape=(jax.ShapeDtypeStruct((2, 4), F32), jax....]
where the time goes in v3:
time: 65.2 us; the launch traced here: 65.1 us
  Pallas kernels  63.2 us (97%)
  local copies, waits for them, and re-layouts  1.29 us (2%)
    pallas_call x1, Pallas kernels, on_device(): pl.pallas_call(kernel, out_shape=(jax.ShapeDtypeStruct((2, 4), F32), jax....  63.2 us

profile of v3, /device:TPU:1, one launch (start us, length us, event | category | flops | bytes accessed | tf_op | source)
XLA Modules:
  0.0 65.1 jit_solution(16986923984778840555)
XLA Ops:
  0.6 63.2 %shard_map.86 = (f32[2,4]{1,0:T(2,128)S(1)}, f32[90,128]{1,0:T(8,128)S(1)}) custom-call(bf16[128,1024]{1,0:T(8,128)(2,1)} %bitcast.6, f32[1,1024]{1,0:T(1,128)} %bitcast.10, bf16[32,3072]{1,0:T(8,128)(2,1)} %wqkv_hbm.1, bf16[32,1024]{1,0:T(8,128)(2,1)} %wout_hbm.1, bf16[90,1024]{1,0:T(8,128)(2,1)} %bitcast.7, s32[2,16,64]{2,1,0:T(8,128)} %bitcast.9, ...), custom_call_target="tpu_custom_call" | custom-call | tf_op jit(solution)/shard_map/pallas_call | solution.py:451
  63.8 0.7 %copy.10 = f32[90,128]{0,1:T(8,128)} copy(f32[90,128]{1,0:T(8,128)S(1)} %get-tuple-element.5) | data formatting | bytes 92160 | tf_op jit(solution)/shard_map/pallas_call | solution.py:451
  64.5 0.6 copy.12

commit v4 on v3

--- a/solution.py
+++ b/solution.py
@@ -31,8 +31,8 @@
 FAR_FIRST, FAR_SECOND = (0, 2, 3), (CHUNKS - 1,)
 PAIRS = {0: 1}
 ORDER = (
-    ("first", 0), ("first", 2), ("first", 3), ("relay", 4), ("relay", 5), ("again", 0), ("halo", 0), ("again", 2),
-    ("core", 0), ("second", 4), ("again", 3), ("second", 5), ("core", 2), ("truth", 0), ("done", 0), ("heads", 0),
+    ("first", 0), ("greet", 2), ("first", 2), ("first", 3), ("greet", 3), ("relay", 4), ("relay", 5), ("again", 0), ("halo", 0), ("again", 2),
+    ("core", 0), ("greet", 4), ("second", 4), ("again", 3), ("second", 5), ("core", 2), ("truth", 0), ("done", 0), ("heads", 0),
     ("core", 1), ("again", 4), ("core", 3), ("done", 2), ("heads", 2), ("done", 1), ("heads", 1), ("core", 4),
     ("core", 5), ("done", 3), ("heads", 3), ("done", 4), ("out", 4), ("done", 5), ("out", 5),
 )
@@ -62,7 +62,7 @@
     tok_hbm, gain_hbm, wqkv_hbm, wout_hbm, dec_hbm, edge_hbm, truth_hbm,
     score_ref, grad_ref,
     tok_ref, gain_ref, dec_ref, edge_ref, truth_ref, wq, wo, halo, normed, count, att, state, dec, truths, fields, pick, e_all,
-    in_sem, w_ssem, w_rsem, h_ssem, h_rsem, t_ssem, t_rsem, f_ssem, f_rsem, e_ssem, e_rsem,
+    in_sem, w_ssem, w_rsem, h_ssem, h_rsem, t_ssem, t_rsem, f_ssem, f_rsem, e_ssem, e_rsem, near_sem,
 ):
     z = lax.axis_index("member")
     p = lax.axis_index("mp")
@@ -93,7 +93,7 @@
 
     barrier = pltpu.get_barrier_semaphore()
     partners = [at_xp, at_xm, at_yp, at_ym, at_x2, at_y2, sib, low, high]
-    partners += [(other(k), p) for k in range(-REACH, REACH + 1) if k]
+    partners += [(other(k), p) for k in (-1, 1)]
     for target in partners:
         pl.semaphore_signal(barrier, inc=1, device_id=target, device_id_type=MESH)
 
@@ -251,10 +251,18 @@
         else:
             arrive(opposite, ssem.at[12], rsem.at[12])
 
+    def greet(n):
+        if n > 1:
+            pl.semaphore_wait(near_sem.at[n - 2, 0], 1)
+            pl.semaphore_wait(near_sem.at[n - 2, 1], 1)
+        if n < REACH:
+            pl.semaphore_signal(near_sem.at[n - 1, 0], inc=1, device_id=up, device_id_type=MESH)
+            pl.semaphore_signal(near_sem.at[n - 1, 1], inc=1, device_id=down, device_id_type=MESH)
+
     go(0, "start")
     for j in gathered[1:]:
         go(j, "start")
-    reach(truths, t_ssem, t_rsem)
+    greet(1)
 
     def norm(rows):
         return (rms_scale(rows[...].astype(F32)) * gain_ref[...]).astype(BF16)
@@ -305,6 +313,11 @@
         if step == "halo":
             send(tok_ref, halo.at[1], h_ssem.at[1], h_rsem.at[1], low)
             send(tok_ref, halo.at[0], h_ssem.at[0], h_rsem.at[0], high)
+            continue
+        if step == "greet":
+            greet(j)
+            if j == REACH:
+                reach(truths, t_ssem, t_rsem)
             continue
         if step == "truth":
             relay(truths, t_ssem, t_rsem)
@@ -482,6 +495,7 @@
             dma((4 * REACH + 1,)),
             dma((2,)),
             dma((2,)),
+            pltpu.SemaphoreType.REGULAR((REACH - 1, 2)),
         ],
         compiler_params=pltpu.CompilerParams(
             collective_id=0, has_side_effects=True, vmem_limit_bytes=48 * 1024 * 1024

time: 65.2 us -> 67.6 us (1.037)
  Pallas kernels: 63.2 us -> 65.5 us
    pallas_call x1, Pallas kernels: 63.2 us -> 65.5 us  [on_device(): pl.pallas_call(kernel, out_shape=(jax.ShapeDtypeStruct((2, 4), F32), jax....]
where the time goes in v4:
time: 67.6 us; the launch traced here: 67.5 us
  Pallas kernels  65.5 us (97%)
  local copies, waits for them, and re-layouts  1.29 us (2%)
    pallas_call x1, Pallas kernels, on_device(): pl.pallas_call(kernel, out_shape=(jax.ShapeDtypeStruct((2, 4), F32), jax....  65.5 us

profile of v4, /device:TPU:1, one launch (start us, length us, event | category | flops | bytes accessed | tf_op | source)
XLA Modules:
  0.0 67.5 jit_solution(15091114235034610774)
XLA Ops:
  0.6 65.5 %shard_map.86 = (f32[2,4]{1,0:T(2,128)S(1)}, f32[90,128]{1,0:T(8,128)S(1)}) custom-call(bf16[128,1024]{1,0:T(8,128)(2,1)} %bitcast.6, f32[1,1024]{1,0:T(1,128)} %bitcast.10, bf16[32,3072]{1,0:T(8,128)(2,1)} %wqkv_hbm.1, bf16[32,1024]{1,0:T(8,128)(2,1)} %wout_hbm.1, bf16[90,1024]{1,0:T(8,128)(2,1)} %bitcast.7, s32[2,16,64]{2,1,0:T(8,128)} %bitcast.9, ...), custom_call_target="tpu_custom_call" | custom-call | tf_op jit(solution)/shard_map/pallas_call | solution.py:464
  66.2 0.7 %copy.10 = f32[90,128]{0,1:T(8,128)} copy(f32[90,128]{1,0:T(8,128)S(1)} %get-tuple-element.5) | data formatting | bytes 92160 | tf_op jit(solution)/shard_map/pallas_call | solution.py:464
  66.9 0.6 copy.12
